TPU v7x, 32 devices: a whole 2x2x4 slice. The times are simulated.
32 devices in a mesh: groups: 2 (over y), ra: 4 (over z), dec: 2 (over x), band: 2 (over core).
Axes of the slice: x: 2, y: 2, z: 4, core: 2. Of those that a mesh axis runs over, the one named last changes fastest.
Arguments:
- sky_maps: bfloat16 [512, 312, 256], P(('groups', 'band'), 'ra', 'dec'), parts along dimension 0, may hold values from -12 to 12
- radii: int32 [512], P(('groups', 'band')), parts along dimension 0, may hold values from 1 to 17, as said below
- valid: int32 [624, 256], P(('groups', 'ra'), 'dec'), parts along dimension 0, may hold values from 0 to 1, as said below
Outputs:
- smoothed: bfloat16 [512, 312, 256], P(('groups', 'band'), 'ra', 'dec'), parts along dimension 0
- channel_mean: float32 [512], P(('groups', 'band')), parts along dimension 0
- covariance: float32 [512, 256], P('groups', 'band'), parts along dimension 0
There are 2 independent parts, one for each index of `groups`. A program takes and returns all parts, laid end to end along the dimension named above; each array names one. Nothing has to cross between parts.
Inputs may be any that keep to these rules, and one draw needn't show every extreme that they name: `radii`: some channel has half-width exactly 17. 1 marks a pixel that enters the statistics; the pixel with declination index 0 is valid in every row.
All inputs are finite; a program needn't handle non-finite values.
Results may differ from a plain program's by a relative error of at most 0.012.
The roundings to bfloat16 on the way count: a program that leaves them out, or rounds other values in their place, can miss the bound.
Values may be sent and summed in bfloat16 or wider, within the bound.
A program may use at most 64 MiB of HBM per device.

v0:
```python
import functools

import jax
import jax.numpy as jnp
from jax import lax
from jax.experimental import pallas as pl
from jax.experimental.pallas import tpu as pltpu
from jax.sharding import PartitionSpec as P

RMAX = 17
WIDE = RMAX + 1
CB = 16
MESH = pl.DeviceIdType.MESH


def up(value, step):
    return -(-value // step) * step


def iota(shape, dim):
    return lax.broadcasted_iota(jnp.int32, shape, dim)


def inner_rows(rows):
    first = RMAX // 16 * 16
    last = up(rows - RMAX, 16)
    return first, last - first, up(RMAX, 8)


def kernel(
    dims, radii_ref, sky_hbm, valid_hbm, out_ref, mean_ref, cov_ref,
    sky_ref, valid_ref, loads,
    tab_dec, tab_in, tab_ed, xs, hs, os, ps, vb, mine_in, mine_ed, other_in, other_ed,
    pack_up, pack_dn, halo_lo, halo_hi, edge_lo, edge_hi, z_before, z_after,
    acc, shares, total, aux, aux_all,
    s_dec, r_dec, s_ra, r_ra, s_band, r_band, s_rs, r_rs, s_ag, r_ag, s_aux, r_aux,
):
    n_ra, n_dec, rows, chans, cols = dims
    blocks = chans // CB
    rows8 = up(rows, 16)
    groups = cols // WIDE
    per = -(-rows // groups)
    peers = n_ra * n_dec
    reducers = min(peers, chans // 8)
    share = chans // reducers
    ext = 128
    in_at, in_rows, edge_rows = inner_rows(rows)
    ra, dec, band = lax.axis_index("ra"), lax.axis_index("dec"), lax.axis_index("band")
    rank = ra * n_dec + dec
    nxt, prv = lax.rem(ra + 1, n_ra), lax.rem(ra + n_ra - 1, n_ra)
    twin = {"band": 1 - band}

    def peer_id(p):
        return {"ra": p // n_dec, "dec": lax.rem(p, n_dec)}

    def each_peer(body):
        def step(d, carry):
            body(lax.rem(rank + d, peers))
            return carry
        lax.fori_loop(1, peers, step, 0)

    def table(r, carry):
        radius = r.astype(jnp.float32)
        spread = 0.5 * radius
        k = lax.rem(iota((8, cols), 0) - iota((8, cols), 1) + cols + cols // 2, cols) - cols // 2
        k = k.astype(jnp.float32)
        raw = jnp.where(jnp.abs(k) <= radius, jnp.exp(-(k * k) / (2.0 * spread * spread)), 0.0)
        first = raw / jnp.sum(raw, axis=1, keepdims=True)
        full = jnp.concatenate([pltpu.roll(first, 8 * t, 1) for t in range(cols // 8)], axis=0)
        near = jnp.abs(iota((cols, cols), 0) - iota((cols, cols), 1)) <= cols // 2
        tab_in[r] = full[in_at:in_at + in_rows].astype(jnp.bfloat16)
        ends = jnp.concatenate([full[0:edge_rows], full[rows8 - edge_rows:rows8]], axis=0)
        tab_ed[r] = ends.astype(jnp.bfloat16)
        tab_dec[r, 0:cols, :] = jnp.where(near, full, 0.0).astype(jnp.bfloat16)
        tab_dec[r, cols:2 * cols, :] = jnp.where(near, 0.0, full).astype(jnp.bfloat16)
        return carry

    load_sky = pltpu.make_async_copy(sky_hbm, sky_ref, loads.at[0])
    load_valid = pltpu.make_async_copy(valid_hbm, valid_ref, loads.at[1])
    load_sky.start()
    load_valid.start()
    barrier = pltpu.get_barrier_semaphore()
    each_peer(lambda p: pl.semaphore_signal(barrier, inc=1, device_id=peer_id(p), device_id_type=MESH))
    pl.semaphore_signal(barrier, inc=1, device_id=twin, device_id_type=MESH)
    lax.fori_loop(1, RMAX + 1, table, 0)
    load_sky.wait()
    pl.semaphore_wait(barrier, peers)

    def remote(src, dst, send, recv, target):
        return pltpu.make_async_remote_copy(
            src_ref=src, dst_ref=dst, send_sem=send, recv_sem=recv, device_id=target, device_id_type=MESH
        )

    def dec_up(b):
        return remote(pack_up.at[b], halo_lo.at[b], s_dec.at[0, b], r_dec.at[0, b], {"dec": dec + 1})

    def dec_dn(b):
        return remote(pack_dn.at[b], halo_hi.at[b], s_dec.at[1, b], r_dec.at[1, b], {"dec": dec - 1})

    def ra_up(b):
        return remote(edge_hi.at[b], z_before.at[b], s_ra.at[0, b], r_ra.at[0, b], {"ra": nxt})

    def ra_dn(b):
        return remote(edge_lo.at[b], z_after.at[b], s_ra.at[1, b], r_ra.at[1, b], {"ra": prv})

    def to_twin(k, b):
        mine, other = ((mine_ed, other_ed), (mine_in, other_in))[k]
        return remote(mine.at[b], other.at[b], s_band.at[k, b], r_band.at[k, b], twin)

    has_hi, has_lo = dec < n_dec - 1, dec > 0
    lanes = iota((1, 1, cols), 2)
    inner = rows - 2 * RMAX
    order = [*range(RMAX), *range(rows - RMAX, rows), *range(RMAX, rows - RMAX)]
    tall = per * groups
    xs[...] = jnp.zeros_like(xs)
    hs[...] = jnp.zeros_like(hs)

    def load_block(b):
        at = pl.multiple_of(b * CB, CB)
        block = sky_ref[:, pl.ds(at, CB), :].astype(jnp.float32)
        xs[0:rows * CB, :] = block.reshape(rows * CB, cols)

    def pack_block(b):
        at = pl.multiple_of(b * CB, CB)

        def packed(first):
            result = jnp.zeros((per, CB, cols), jnp.float32)
            for g in range(groups):
                end = min(rows, (g + 1) * per)
                part = sky_ref[g * per:end, pl.ds(at, CB), :].astype(jnp.float32)
                if end < (g + 1) * per:
                    fill = jnp.zeros(((g + 1) * per - end, CB, cols), jnp.float32)
                    part = jnp.concatenate([part, fill], axis=0)
                turned = pltpu.roll(part, (WIDE * g - first) % cols, 2)
                inside = (lanes >= WIDE * g) & (lanes < WIDE * (g + 1))
                result = jnp.where(inside, turned, result)
            return result.astype(jnp.bfloat16)

        @pl.when(has_hi)
        def _():
            pack_up[b] = packed(cols - WIDE)
            dec_up(b).start()

        @pl.when(has_lo)
        def _():
            pack_dn[b] = packed(0)
            dec_dn(b).start()

    ahead = min(2, blocks)
    for b in range(ahead):
        pack_block(jnp.int32(b))

    load_valid.wait()
    weights = valid_ref[...].astype(jnp.float32)
    for at, x in enumerate(order):
        vb[at] = jnp.broadcast_to(weights[x:x + 1, :], (CB, cols)).astype(jnp.bfloat16)

    def unpack(b, side):
        low = None if side == "high" else halo_lo[b].astype(jnp.float32)
        high = None if side == "low" else halo_hi[b].astype(jnp.float32)
        for g in range(groups):
            if side != "high":
                left = pltpu.roll(low, (cols - WIDE - WIDE * g) % cols, 2)
            if side != "low":
                right = pltpu.roll(high, (-WIDE * g) % cols, 2)
            on_right = lanes < cols // 2
            if side == "both":
                both = jnp.where(on_right, right, left)
            elif side == "low":
                both = jnp.where(on_right, 0.0, left)
            else:
                both = jnp.where(on_right, right, 0.0)
            hs[g * per * CB:(g + 1) * per * CB, :] = both.reshape(per * CB, cols)

    def for_blocks(body):
        def step(b, carry):
            body(b)
            return carry
        lax.fori_loop(0, blocks, step, 0)

    def smooth_rows(b, tab, height):
        for c in range(CB):
            rr = radii_ref[b * CB + c]
            column = ps[b, pl.ds(c, ext, stride=CB), :].astype(jnp.bfloat16)
            os[pl.ds(c, height, stride=CB), :] = jnp.dot(
                tab[rr], column, preferred_element_type=jnp.float32
            )

    def gram_of(mine, other, first, height):
        steps = next(n for n in (8, 6, 4, 2, 1) if height % n == 0)
        if height % 34 == 0:
            steps = 34
        if height % 22 == 0:
            steps = 22

        def gram(i, carry):
            def row(ref, x):
                return ref[:, pl.ds(x, 1), :, :].reshape(chans, cols)

            own = jnp.concatenate([row(mine, i * steps + s) for s in range(steps)], axis=1)
            oth = jnp.concatenate([row(other, i * steps + s) for s in range(steps)], axis=1)
            msk = jnp.concatenate([vb[first + i * steps + s] for s in range(steps)], axis=1)
            acc[...] += lax.dot_general(
                jnp.concatenate([own, msk], axis=0), jnp.concatenate([own, oth], axis=0),
                (((1,), (1,)), ((), ())), preferred_element_type=jnp.float32,
            )
            return carry

        lax.fori_loop(0, height // steps, gram, 0)

    def dec_block(b, carry):
        @pl.when(b + ahead < blocks)
        def _():
            pack_block(b + ahead)

        load_block(b)
        ps[b, rows8 * CB:ext * CB, :] = jnp.zeros(((ext - rows8) * CB, cols), jnp.float32)

        @pl.when(has_lo)
        def _():
            dec_up(b).wait_recv()

        @pl.when(has_hi)
        def _():
            dec_dn(b).wait_recv()

        @pl.when(has_lo & has_hi)
        def _():
            unpack(b, "both")

        @pl.when(has_lo & jnp.logical_not(has_hi))
        def _():
            unpack(b, "low")

        @pl.when(has_hi & jnp.logical_not(has_lo))
        def _():
            unpack(b, "high")

        for c in range(CB):
            rr = radii_ref[b * CB + c]
            main = xs[pl.ds(c, rows8, stride=CB), :]
            side = hs[pl.ds(c, rows8, stride=CB), :]
            left_hand = jnp.concatenate([main, side], axis=1).astype(jnp.bfloat16)
            part = jnp.dot(left_hand, tab_dec[rr], preferred_element_type=jnp.float32)
            part = part.astype(jnp.bfloat16).astype(jnp.float32)
            ps[b, pl.ds(c, rows8, stride=CB), :] = part
        edge_lo[b] = ps[b, 0:RMAX * CB, :].reshape(RMAX, CB, cols).astype(jnp.bfloat16)
        last = ps[b, (rows - RMAX) * CB:rows * CB, :]
        edge_hi[b] = last.reshape(RMAX, CB, cols).astype(jnp.bfloat16)
        ra_up(b).start()
        ra_dn(b).start()
        smooth_rows(b, tab_in, in_rows)
        at = RMAX - in_at
        smooth = os[at * CB:(at + inner) * CB, :].reshape(inner, CB, cols).astype(jnp.bfloat16)
        out_ref[RMAX:rows - RMAX, pl.ds(pl.multiple_of(b * CB, CB), CB), :] = smooth
        mine_in[b] = smooth * vb[2 * RMAX:rows]
        to_twin(1, b).start()
        return carry

    lax.fori_loop(0, blocks, dec_block, 0)
    for_blocks(lambda b: to_twin(1, b).wait_recv())
    acc[...] = jnp.zeros_like(acc)
    gram_of(mine_in, other_in, 2 * RMAX, inner)

    def ra_block(b, carry):
        ra_up(b).wait_recv()
        ra_dn(b).wait_recv()
        before = z_before[b].astype(jnp.float32)
        ps[b, (ext - RMAX) * CB:ext * CB, :] = before.reshape(RMAX * CB, cols)
        after = z_after[b].astype(jnp.float32)
        ps[b, rows * CB:(rows + RMAX) * CB, :] = after.reshape(RMAX * CB, cols)
        smooth_rows(b, tab_ed, 2 * edge_rows)
        low = os[0:RMAX * CB, :].reshape(RMAX, CB, cols).astype(jnp.bfloat16)
        at = 2 * edge_rows - rows8 + rows - RMAX
        high = os[at * CB:(at + RMAX) * CB, :].reshape(RMAX, CB, cols).astype(jnp.bfloat16)
        here = pl.ds(pl.multiple_of(b * CB, CB), CB)
        out_ref[0:RMAX, here, :] = low
        out_ref[rows - RMAX:rows, here, :] = high
        mine_ed[b, 0:RMAX] = low * vb[0:RMAX]
        mine_ed[b, RMAX:2 * RMAX] = high * vb[RMAX:2 * RMAX]
        to_twin(0, b).start()
        return carry

    lax.fori_loop(0, blocks, ra_block, 0)
    for_blocks(lambda b: to_twin(0, b).wait_recv())
    gram_of(mine_ed, other_ed, 0, 2 * RMAX)
    count = jnp.sum(weights, keepdims=True)
    aux[...] = jnp.where(iota((8, 2 * chans), 0) == 0, acc[chans:chans + 8, :], count)

    def part_of(p):
        return acc.at[pl.ds(pl.multiple_of(p * share, share), share), :]

    def rs(p, slot):
        return remote(part_of(p), shares.at[slot], s_rs.at[p], r_rs.at[slot], peer_id(p))

    def ag(p, slot):
        mypart = total.at[pl.ds(pl.multiple_of(slot * share, share), share), :]
        return remote(mypart, mypart, s_ag.at[p], r_ag.at[slot], peer_id(p))

    def au(p, slot):
        return remote(aux, aux_all.at[slot], s_aux.at[p], r_aux.at[slot], peer_id(p))

    def reducing(p, body):
        if reducers == peers:
            body()
        else:
            pl.when(p < reducers)(body)

    each_peer(lambda p: reducing(p, lambda: rs(p, rank).start()))
    each_peer(lambda p: au(p, rank).start())
    aux_all[rank] = aux[...]

    def reduce_own():
        shares[rank] = acc[pl.ds(pl.multiple_of(rank * share, share), share), :]
        each_peer(lambda p: rs(rank, p).wait_recv())
        whole = shares[0]
        whole = lax.fori_loop(1, peers, lambda p, t: t + shares[p], whole)
        total[pl.ds(pl.multiple_of(rank * share, share), share), :] = whole
        each_peer(lambda p: ag(p, rank).start())

    reducing(rank, reduce_own)
    each_peer(lambda p: au(p, p).wait_recv())
    sums = lax.fori_loop(1, peers, lambda p, t: t + aux_all[p], aux_all[0])
    count = sums[1:2, 0:1]
    means = sums[0:1, :] / count
    mean_ref[...] = means[:, 0:chans]
    column = jnp.transpose(jnp.broadcast_to(means[:, 0:chans], (chans, chans)))
    each_peer(lambda p: reducing(p, lambda: ag(p, p).wait_recv()))
    for k in range(2):
        across = means[:, k * chans:(k + 1) * chans]
        block = (total[:, k * chans:(k + 1) * chans] - count * column * across) / (count - 1.0)
        place = band if k == 0 else 1 - band
        cov_ref[pl.ds(pl.multiple_of(place * chans, chans), chans), :] = jnp.transpose(block)

    def finish(b, carry):
        pl.when(has_hi)(lambda: dec_up(b).wait_send())
        pl.when(has_lo)(lambda: dec_dn(b).wait_send())
        ra_up(b).wait_send()
        ra_dn(b).wait_send()
        to_twin(0, b).wait_send()
        to_twin(1, b).wait_send()
        return carry

    lax.fori_loop(0, blocks, finish, 0)
    each_peer(lambda p: reducing(p, lambda: rs(p, rank).wait_send()))
    each_peer(lambda p: au(p, rank).wait_send())
    reducing(rank, lambda: each_peer(lambda p: ag(p, rank).wait_send()))


def per_device(n_ra, n_dec, sky_maps, radii, valid):
    chans, rows, cols = sky_maps.shape
    blocks = chans // CB
    rows8 = up(rows, 16)
    groups = cols // WIDE
    per = -(-rows // groups)
    peers = n_ra * n_dec
    share = chans // min(peers, chans // 8)
    tall = max(per * groups, rows8)
    f32, b16, dma = jnp.float32, jnp.bfloat16, pltpu.SemaphoreType.DMA
    vmem = pl.BlockSpec(memory_space=pltpu.VMEM)
    hbm = pl.BlockSpec(memory_space=pltpu.HBM)
    in_at, in_rows, edge_rows = inner_rows(rows)
    inner, outer = rows - 2 * RMAX, 2 * RMAX
    flat = jnp.transpose(sky_maps, (1, 0, 2))
    packed = pltpu.VMEM((blocks, per, CB, cols), b16)
    edge = pltpu.VMEM((blocks, RMAX, CB, cols), b16)
    smoothed, mean, cov = pl.pallas_call(
        functools.partial(kernel, (n_ra, n_dec, rows, chans, cols)),
        out_shape=(
            jax.ShapeDtypeStruct((rows, chans, cols), b16),
            jax.ShapeDtypeStruct((1, chans), f32),
            jax.ShapeDtypeStruct((2 * chans, chans), f32),
        ),
        in_specs=[pl.BlockSpec(memory_space=pltpu.SMEM), hbm, hbm],
        out_specs=(vmem, vmem, vmem),
        scratch_shapes=[
            pltpu.VMEM((rows, chans, cols), b16),
            pltpu.VMEM((rows, cols), jnp.int32),
            dma((2,)),
            pltpu.VMEM((RMAX + 1, 2 * cols, cols), b16),
            pltpu.VMEM((RMAX + 1, in_rows, 128), b16),
            pltpu.VMEM((RMAX + 1, 2 * edge_rows, 128), b16),
            pltpu.VMEM((tall * CB, cols), f32),
            pltpu.VMEM((tall * CB, cols), f32),
            pltpu.VMEM((rows8 * CB, cols), f32),
            pltpu.VMEM((blocks, 128 * CB, cols), f32),
            pltpu.VMEM((rows, CB, cols), b16),
            pltpu.VMEM((blocks, inner, CB, cols), b16),
            pltpu.VMEM((blocks, outer, CB, cols), b16),
            pltpu.VMEM((blocks, inner, CB, cols), b16),
            pltpu.VMEM((blocks, outer, CB, cols), b16),
            packed, packed, packed, packed,
            edge, edge, edge, edge,
            pltpu.VMEM((chans + CB, 2 * chans), f32),
            pltpu.VMEM((peers, share, 2 * chans), f32),
            pltpu.VMEM((chans, 2 * chans), f32),
            pltpu.VMEM((8, 2 * chans), f32),
            pltpu.VMEM((peers, 8, 2 * chans), f32),
            dma((2, blocks)), dma((2, blocks)), dma((2, blocks)), dma((2, blocks)),
            dma((2, blocks)), dma((2, blocks)),
            dma((peers,)), dma((peers,)), dma((peers,)), dma((peers,)), dma((peers,)), dma((peers,)),
        ],
        compiler_params=pltpu.CompilerParams(
            collective_id=0, has_side_effects=True, vmem_limit_bytes=32 * 1024 * 1024
        ),
    )(radii, flat, valid)
    return (jnp.transpose(smoothed, (1, 0, 2)), mean.reshape(chans), cov)


def solution(mesh):
    return jax.shard_map(
        functools.partial(per_device, mesh.shape["ra"], mesh.shape["dec"]),
        mesh=mesh,
        in_specs=(
            P(("groups", "band"), "ra", "dec"),
            P(("groups", "band")),
            P(("groups", "ra"), "dec"),
        ),
        out_specs=(P(("groups", "band"), "ra", "dec"), P(("groups", "band")), P("groups", "band")),
        check_vma=False,
    )
```

profile of v0, /device:TPU:0, one launch (start us, length us, event | category | flops | bytes accessed | tf_op | source)
XLA Modules:
  0.0 56.5 jit_solution(5631129201603299532)
XLA Ops:
  0.6 0.0 copy-start
  0.6 1.7 %copy-done = bf16[128,78,128]{2,0,1:T(8,128)(2,1)S(1)} copy-done((bf16[128,78,128]{2,0,1:T(8,128)(2,1)S(1)}, bf16[128,78,128]{2,0,1:T(8,128)(2,1)}, u32[]{:S(2)}) %copy-start) | copy-done | bytes 2555928
  2.4 0.0 copy-start.1
  2.4 0.8 %copy-done.1 = s32[78,128]{1,0:T(8,128)S(1)} copy-done((s32[78,128]{1,0:T(8,128)S(1)}, s32[78,128]{1,0:T(8,128)}, u32[]{:S(2)}) %copy-start.1) | copy-done | bytes 39960
  3.1 0.0 copy-start.2
  3.1 0.7 %copy-done.2 = s32[128]{0:T(128)S(1)} copy-done((s32[128]{0:T(128)S(1)}, s32[128]{0:T(128)}, u32[]{:S(2)}) %copy-start.2) | copy-done | bytes 536
  3.8 50.1 %shard_map.58 = (bf16[78,128,128]{2,1,0:T(8,128)(2,1)S(1)}, f32[1,128]{1,0:T(1,128)S(1)}, f32[256,128]{1,0:T(8,128)S(1)}) custom-call(s32[128]{0:T(128)S(1)} %copy-done.2, bf16[78,128,128]{2,1,0:T(8,128)(2,1)S(1)} %bitcast.3, s32[78,128]{1,0:T(8,128)S(1)} %copy-done.1), custom_call_target="tpu_custom_call" | custom-call | tf_op jit(solution)/shard_map/pallas_call | solution.py:367
  53.9 1.5 %copy.9 = bf16[128,78,128]{2,0,1:T(8,128)(2,1)} copy(bf16[128,78,128]{2,0,1:T(8,128)(2,1)S(1)} %bitcast.4) | data formatting | bytes 5111808
  55.3 0.5 copy.10
  55.9 0.7 %copy.11 = f32[256,128]{1,0:T(8,128)} copy(f32[256,128]{1,0:T(8,128)S(1)} %get-tuple-element.14) | data formatting | bytes 262144
Async XLA Ops:
  0.6 1.7 %copy-start = (bf16[128,78,128]{2,0,1:T(8,128)(2,1)S(1)}, bf16[128,78,128]{2,0,1:T(8,128)(2,1)}, u32[]{:S(2)}) copy-start(bf16[128,78,128]{2,0,1:T(8,128)(2,1)} %param.3) | copy-start | bytes 7667716
  2.4 0.8 %copy-start.1 = (s32[78,128]{1,0:T(8,128)S(1)}, s32[78,128]{1,0:T(8,128)}, u32[]{:S(2)}) copy-start(s32[78,128]{1,0:T(8,128)} %valid_hbm.1) | copy-start | bytes 119812
  3.1 0.7 %copy-start.2 = (s32[128]{0:T(128)S(1)}, s32[128]{0:T(128)}, u32[]{:S(2)}) copy-start(s32[128]{0:T(128)} %radii_ref.1) | copy-start | bytes 1540
where the time goes:
time: 56.7 us; the launch traced here: 56.5 us
  Pallas kernels  50.1 us (88%)
  local copies, waits for them, and re-layouts  5.79 us (10%)
  between operations  0.65 us (1%)
    pallas_call x1, Pallas kernels, per_device(): pl.pallas_call(functools.partial(kernel, (n_ra, n_dec, rows, chans, cols)...  50.1 us
    unnamed x9, local copies, waits for them, and re-layouts  5.79 us

commit v1 on v0

--- a/solution.py
+++ b/solution.py
@@ -10,6 +10,7 @@
 RMAX = 17
 WIDE = RMAX + 1
 CB = 16
+EARLY = 2
 MESH = pl.DeviceIdType.MESH
 
 
@@ -19,6 +20,10 @@
 
 def iota(shape, dim):
     return lax.broadcasted_iota(jnp.int32, shape, dim)
+
+
+def early_blocks(blocks):
+    return min(EARLY, blocks - 1)
 
 
 def inner_rows(rows):
@@ -28,10 +33,10 @@
 
 
 def kernel(
-    dims, radii_ref, sky_hbm, valid_hbm, out_ref, mean_ref, cov_ref,
-    sky_ref, valid_ref, loads,
+    dims, radii_hbm, sky_hbm, valid_hbm, out_ref, mean_ref, cov_ref,
+    sky_ref, valid_ref, radii_ref, loads,
     tab_dec, tab_in, tab_ed, xs, hs, os, ps, vb, mine_in, mine_ed, other_in, other_ed,
-    pack_up, pack_dn, halo_lo, halo_hi, edge_lo, edge_hi, z_before, z_after,
+    pack_up, pack_dn, halo_lo, halo_hi, far_up, far_dn, far_lo, far_hi, edge_lo, edge_hi, z_before, z_after,
     acc, shares, total, aux, aux_all,
     s_dec, r_dec, s_ra, r_ra, s_band, r_band, s_rs, r_rs, s_ag, r_ag, s_aux, r_aux,
 ):
@@ -40,6 +45,8 @@
     rows8 = up(rows, 16)
     groups = cols // WIDE
     per = -(-rows // groups)
+    far_per = -(-2 * RMAX // groups)
+    late = blocks - early_blocks(blocks)
     peers = n_ra * n_dec
     reducers = min(peers, chans // 8)
     share = chans // reducers
@@ -75,15 +82,27 @@
         tab_dec[r, cols:2 * cols, :] = jnp.where(near, 0.0, full).astype(jnp.bfloat16)
         return carry
 
-    load_sky = pltpu.make_async_copy(sky_hbm, sky_ref, loads.at[0])
-    load_valid = pltpu.make_async_copy(valid_hbm, valid_ref, loads.at[1])
-    load_sky.start()
-    load_valid.start()
+    def load_sky(b):
+        at = pl.multiple_of(b * CB, CB)
+        return pltpu.make_async_copy(
+            sky_hbm.at[:, pl.ds(at, CB), :], sky_ref.at[:, pl.ds(at, CB), :], loads.at[b]
+        )
+
+    load_valid = pltpu.make_async_copy(valid_hbm, valid_ref, loads.at[blocks])
+    load_radii = pltpu.make_async_copy(radii_hbm, radii_ref, loads.at[blocks + 1])
     barrier = pltpu.get_barrier_semaphore()
     each_peer(lambda p: pl.semaphore_signal(barrier, inc=1, device_id=peer_id(p), device_id_type=MESH))
     pl.semaphore_signal(barrier, inc=1, device_id=twin, device_id_type=MESH)
-    lax.fori_loop(1, RMAX + 1, table, 0)
-    load_sky.wait()
+
+    def for_blocks(body, first=0, last=blocks):
+        def step(b, carry):
+            body(b)
+            return carry
+        lax.fori_loop(first, last, step, 0)
+
+    for_blocks(lambda b: load_sky(b).start())
+    load_valid.start()
+    load_radii.start()
     pl.semaphore_wait(barrier, peers)
 
     def remote(src, dst, send, recv, target):
@@ -97,6 +116,24 @@
     def dec_dn(b):
         return remote(pack_dn.at[b], halo_hi.at[b], s_dec.at[1, b], r_dec.at[1, b], {"dec": dec - 1})
 
+    def far_dec_up(j):
+        return remote(
+            far_up.at[j], far_lo.at[j], s_dec.at[0, blocks + j], r_dec.at[0, blocks + j], {"dec": dec + 1}
+        )
+
+    def far_dec_dn(j):
+        return remote(
+            far_dn.at[j], far_hi.at[j], s_dec.at[1, blocks + j], r_dec.at[1, blocks + j], {"dec": dec - 1}
+        )
+
+    def sky_up(b):
+        rim = sky_hbm.at[pl.ds(rows - RMAX, RMAX), pl.ds(pl.multiple_of(b * CB, CB), CB), :]
+        return remote(rim, z_before.at[b], s_ra.at[0, b], r_ra.at[0, b], {"ra": nxt})
+
+    def sky_dn(b):
+        rim = sky_hbm.at[pl.ds(0, RMAX), pl.ds(pl.multiple_of(b * CB, CB), CB), :]
+        return remote(rim, z_after.at[b], s_ra.at[1, b], r_ra.at[1, b], {"ra": prv})
+
     def ra_up(b):
         return remote(edge_hi.at[b], z_before.at[b], s_ra.at[0, b], r_ra.at[0, b], {"ra": nxt})
 
@@ -111,53 +148,89 @@
     lanes = iota((1, 1, cols), 2)
     inner = rows - 2 * RMAX
     order = [*range(RMAX), *range(rows - RMAX, rows), *range(RMAX, rows - RMAX)]
-    tall = per * groups
-    xs[...] = jnp.zeros_like(xs)
-    hs[...] = jnp.zeros_like(hs)
+
+    def send_sky(b):
+        sky_up(b).start()
+        sky_dn(b).start()
+
+    for_blocks(send_sky, late)
 
     def load_block(b):
         at = pl.multiple_of(b * CB, CB)
         block = sky_ref[:, pl.ds(at, CB), :].astype(jnp.float32)
         xs[0:rows * CB, :] = block.reshape(rows * CB, cols)
 
+    def packed(read, count, deep, first):
+        result = jnp.zeros((deep, CB, cols), jnp.float32)
+        for g in range(-(-count // deep)):
+            end = min(count, (g + 1) * deep)
+            part = read(g * deep, end).astype(jnp.float32)
+            if end < (g + 1) * deep:
+                fill = jnp.zeros(((g + 1) * deep - end, CB, cols), jnp.float32)
+                part = jnp.concatenate([part, fill], axis=0)
+            turned = pltpu.roll(part, (WIDE * g - first) % cols, 2)
+            inside = (lanes >= WIDE * g) & (lanes < WIDE * (g + 1))
+            result = jnp.where(inside, turned, result)
+        return result.astype(jnp.bfloat16)
+
     def pack_block(b):
+        load_sky(b).wait()
         at = pl.multiple_of(b * CB, CB)
 
-        def packed(first):
-            result = jnp.zeros((per, CB, cols), jnp.float32)
-            for g in range(groups):
-                end = min(rows, (g + 1) * per)
-                part = sky_ref[g * per:end, pl.ds(at, CB), :].astype(jnp.float32)
-                if end < (g + 1) * per:
-                    fill = jnp.zeros(((g + 1) * per - end, CB, cols), jnp.float32)
-                    part = jnp.concatenate([part, fill], axis=0)
-                turned = pltpu.roll(part, (WIDE * g - first) % cols, 2)
-                inside = (lanes >= WIDE * g) & (lanes < WIDE * (g + 1))
-                result = jnp.where(inside, turned, result)
-            return result.astype(jnp.bfloat16)
+        def read(first, last):
+            return sky_ref[first:last, pl.ds(at, CB), :]
 
         @pl.when(has_hi)
         def _():
-            pack_up[b] = packed(cols - WIDE)
+            pack_up[b] = packed(read, rows, per, cols - WIDE)
             dec_up(b).start()
 
         @pl.when(has_lo)
         def _():
-            pack_dn[b] = packed(0)
+            pack_dn[b] = packed(read, rows, per, 0)
             dec_dn(b).start()
+
+    def pack_far(j):
+        b = late + j
+        sky_up(b).wait_recv()
+        sky_dn(b).wait_recv()
+
+        def read(first, last):
+            both = []
+            if first < RMAX:
+                both.append(z_before[b, first:min(last, RMAX)])
+            if last > RMAX:
+                both.append(z_after[b, max(first, RMAX) - RMAX:last - RMAX])
+            return jnp.concatenate(both, axis=0)
+
+        @pl.when(has_hi)
+        def _():
+            far_up[j] = packed(read, 2 * RMAX, far_per, cols - WIDE)
+            far_dec_up(j).start()
+
+        @pl.when(has_lo)
+        def _():
+            far_dn[j] = packed(read, 2 * RMAX, far_per, 0)
+            far_dec_dn(j).start()
 
     ahead = min(2, blocks)
     for b in range(ahead):
         pack_block(jnp.int32(b))
 
+    lax.fori_loop(1, RMAX + 1, table, 0)
+    spare = xs.shape[0] - rows * CB
+    xs[rows * CB:, :] = jnp.zeros((spare, cols), jnp.float32)
+    if n_dec == 1:
+        hs[...] = jnp.zeros_like(hs)
+    load_radii.wait()
     load_valid.wait()
     weights = valid_ref[...].astype(jnp.float32)
     for at, x in enumerate(order):
         vb[at] = jnp.broadcast_to(weights[x:x + 1, :], (CB, cols)).astype(jnp.bfloat16)
 
-    def unpack(b, side):
-        low = None if side == "high" else halo_lo[b].astype(jnp.float32)
-        high = None if side == "low" else halo_hi[b].astype(jnp.float32)
+    def unpack(low_ref, high_ref, deep, side):
+        low = None if side == "high" else low_ref[...].astype(jnp.float32)
+        high = None if side == "low" else high_ref[...].astype(jnp.float32)
         for g in range(groups):
             if side != "high":
                 left = pltpu.roll(low, (cols - WIDE - WIDE * g) % cols, 2)
@@ -170,13 +243,21 @@
                 both = jnp.where(on_right, 0.0, left)
             else:
                 both = jnp.where(on_right, right, 0.0)
-            hs[g * per * CB:(g + 1) * per * CB, :] = both.reshape(per * CB, cols)
-
-    def for_blocks(body):
-        def step(b, carry):
-            body(b)
-            return carry
-        lax.fori_loop(0, blocks, step, 0)
+            hs[g * deep * CB:(g + 1) * deep * CB, :] = both.reshape(deep * CB, cols)
+
+    def unpack_sides(low_ref, high_ref, deep):
+        pl.when(has_lo & has_hi)(lambda: unpack(low_ref, high_ref, deep, "both"))
+        pl.when(has_lo & jnp.logical_not(has_hi))(lambda: unpack(low_ref, high_ref, deep, "low"))
+        pl.when(has_hi & jnp.logical_not(has_lo))(lambda: unpack(low_ref, high_ref, deep, "high"))
+
+    def smooth_columns(b, height, put):
+        for c in range(CB):
+            rr = radii_ref[b * CB + c]
+            main = xs[pl.ds(c, height, stride=CB), :]
+            side = hs[pl.ds(c, height, stride=CB), :]
+            left_hand = jnp.concatenate([main, side], axis=1).astype(jnp.bfloat16)
+            part = jnp.dot(left_hand, tab_dec[rr], preferred_element_type=jnp.float32)
+            put(c, part.astype(jnp.bfloat16).astype(jnp.float32))
 
     def smooth_rows(b, tab, height):
         for c in range(CB):
@@ -216,59 +297,68 @@
         load_block(b)
         ps[b, rows8 * CB:ext * CB, :] = jnp.zeros(((ext - rows8) * CB, cols), jnp.float32)
 
-        @pl.when(has_lo)
-        def _():
-            dec_up(b).wait_recv()
-
-        @pl.when(has_hi)
-        def _():
-            dec_dn(b).wait_recv()
-
-        @pl.when(has_lo & has_hi)
-        def _():
-            unpack(b, "both")
-
-        @pl.when(has_lo & jnp.logical_not(has_hi))
-        def _():
-            unpack(b, "low")
-
-        @pl.when(has_hi & jnp.logical_not(has_lo))
-        def _():
-            unpack(b, "high")
-
-        for c in range(CB):
-            rr = radii_ref[b * CB + c]
-            main = xs[pl.ds(c, rows8, stride=CB), :]
-            side = hs[pl.ds(c, rows8, stride=CB), :]
-            left_hand = jnp.concatenate([main, side], axis=1).astype(jnp.bfloat16)
-            part = jnp.dot(left_hand, tab_dec[rr], preferred_element_type=jnp.float32)
-            part = part.astype(jnp.bfloat16).astype(jnp.float32)
+        pl.when(has_lo)(lambda: dec_up(b).wait_recv())
+        pl.when(has_hi)(lambda: dec_dn(b).wait_recv())
+        unpack_sides(halo_lo.at[b], halo_hi.at[b], per)
+
+        def put(c, part):
             ps[b, pl.ds(c, rows8, stride=CB), :] = part
-        edge_lo[b] = ps[b, 0:RMAX * CB, :].reshape(RMAX, CB, cols).astype(jnp.bfloat16)
-        last = ps[b, (rows - RMAX) * CB:rows * CB, :]
-        edge_hi[b] = last.reshape(RMAX, CB, cols).astype(jnp.bfloat16)
-        ra_up(b).start()
-        ra_dn(b).start()
+
+        smooth_columns(b, rows8, put)
+
+        @pl.when(b < late)
+        def _():
+            edge_lo[b] = ps[b, 0:RMAX * CB, :].reshape(RMAX, CB, cols).astype(jnp.bfloat16)
+            last = ps[b, (rows - RMAX) * CB:rows * CB, :]
+            edge_hi[b] = last.reshape(RMAX, CB, cols).astype(jnp.bfloat16)
+            ra_up(b).start()
+            ra_dn(b).start()
+
         smooth_rows(b, tab_in, in_rows)
         at = RMAX - in_at
         smooth = os[at * CB:(at + inner) * CB, :].reshape(inner, CB, cols).astype(jnp.bfloat16)
         out_ref[RMAX:rows - RMAX, pl.ds(pl.multiple_of(b * CB, CB), CB), :] = smooth
         mine_in[b] = smooth * vb[2 * RMAX:rows]
         to_twin(1, b).start()
+        pl.when(b == late // 2)(lambda: for_blocks(pack_far, 0, blocks - late))
         return carry
 
     lax.fori_loop(0, blocks, dec_block, 0)
+
+    def far_block(j):
+        b = late + j
+        for first, ref in ((0, z_before), (RMAX, z_after)):
+            rim = ref[b].astype(jnp.float32)
+            xs[first * CB:(first + RMAX) * CB, :] = rim.reshape(RMAX * CB, cols)
+        pl.when(has_lo)(lambda: far_dec_up(j).wait_recv())
+        pl.when(has_hi)(lambda: far_dec_dn(j).wait_recv())
+        unpack_sides(far_lo.at[j], far_hi.at[j], far_per)
+        height = up(2 * RMAX, 16)
+
+        def put(c, part):
+            os[pl.ds(c, height, stride=CB), :] = part
+
+        smooth_columns(b, height, put)
+        ps[b, (ext - RMAX) * CB:ext * CB, :] = os[0:RMAX * CB, :]
+        ps[b, rows * CB:(rows + RMAX) * CB, :] = os[RMAX * CB:2 * RMAX * CB, :]
+
+    for_blocks(far_block, 0, blocks - late)
     for_blocks(lambda b: to_twin(1, b).wait_recv())
     acc[...] = jnp.zeros_like(acc)
     gram_of(mine_in, other_in, 2 * RMAX, inner)
 
-    def ra_block(b, carry):
-        ra_up(b).wait_recv()
-        ra_dn(b).wait_recv()
-        before = z_before[b].astype(jnp.float32)
-        ps[b, (ext - RMAX) * CB:ext * CB, :] = before.reshape(RMAX * CB, cols)
-        after = z_after[b].astype(jnp.float32)
-        ps[b, rows * CB:(rows + RMAX) * CB, :] = after.reshape(RMAX * CB, cols)
+    def ra_block(i, carry):
+        b = lax.rem(i + late, blocks)
+
+        @pl.when(b < late)
+        def _():
+            ra_up(b).wait_recv()
+            ra_dn(b).wait_recv()
+            before = z_before[b].astype(jnp.float32)
+            ps[b, (ext - RMAX) * CB:ext * CB, :] = before.reshape(RMAX * CB, cols)
+            after = z_after[b].astype(jnp.float32)
+            ps[b, rows * CB:(rows + RMAX) * CB, :] = after.reshape(RMAX * CB, cols)
+
         smooth_rows(b, tab_ed, 2 * edge_rows)
         low = os[0:RMAX * CB, :].reshape(RMAX, CB, cols).astype(jnp.bfloat16)
         at = 2 * edge_rows - rows8 + rows - RMAX
@@ -332,16 +422,25 @@
         place = band if k == 0 else 1 - band
         cov_ref[pl.ds(pl.multiple_of(place * chans, chans), chans), :] = jnp.transpose(block)
 
-    def finish(b, carry):
+    def finish(b):
         pl.when(has_hi)(lambda: dec_up(b).wait_send())
         pl.when(has_lo)(lambda: dec_dn(b).wait_send())
+        to_twin(0, b).wait_send()
+        to_twin(1, b).wait_send()
+
+    def finish_late(b):
         ra_up(b).wait_send()
         ra_dn(b).wait_send()
-        to_twin(0, b).wait_send()
-        to_twin(1, b).wait_send()
-        return carry
-
-    lax.fori_loop(0, blocks, finish, 0)
+
+    def finish_early(j):
+        sky_up(late + j).wait_send()
+        sky_dn(late + j).wait_send()
+        pl.when(has_hi)(lambda: far_dec_up(j).wait_send())
+        pl.when(has_lo)(lambda: far_dec_dn(j).wait_send())
+
+    for_blocks(finish)
+    for_blocks(finish_late, 0, late)
+    for_blocks(finish_early, 0, blocks - late)
     each_peer(lambda p: reducing(p, lambda: rs(p, rank).wait_send()))
     each_peer(lambda p: au(p, rank).wait_send())
     reducing(rank, lambda: each_peer(lambda p: ag(p, rank).wait_send()))
@@ -355,6 +454,8 @@
     per = -(-rows // groups)
     peers = n_ra * n_dec
     share = chans // min(peers, chans // 8)
+    early = early_blocks(blocks)
+    far_per = -(-2 * RMAX // groups)
     tall = max(per * groups, rows8)
     f32, b16, dma = jnp.float32, jnp.bfloat16, pltpu.SemaphoreType.DMA
     vmem = pl.BlockSpec(memory_space=pltpu.VMEM)
@@ -363,6 +464,7 @@
     inner, outer = rows - 2 * RMAX, 2 * RMAX
     flat = jnp.transpose(sky_maps, (1, 0, 2))
     packed = pltpu.VMEM((blocks, per, CB, cols), b16)
+    far = pltpu.VMEM((early, far_per, CB, cols), b16)
     edge = pltpu.VMEM((blocks, RMAX, CB, cols), b16)
     smoothed, mean, cov = pl.pallas_call(
         functools.partial(kernel, (n_ra, n_dec, rows, chans, cols)),
@@ -371,12 +473,13 @@
             jax.ShapeDtypeStruct((1, chans), f32),
             jax.ShapeDtypeStruct((2 * chans, chans), f32),
         ),
-        in_specs=[pl.BlockSpec(memory_space=pltpu.SMEM), hbm, hbm],
+        in_specs=[hbm, hbm, hbm],
         out_specs=(vmem, vmem, vmem),
         scratch_shapes=[
             pltpu.VMEM((rows, chans, cols), b16),
             pltpu.VMEM((rows, cols), jnp.int32),
-            dma((2,)),
+            pltpu.SMEM((chans,), jnp.int32),
+            dma((blocks + 2,)),
             pltpu.VMEM((RMAX + 1, 2 * cols, cols), b16),
             pltpu.VMEM((RMAX + 1, in_rows, 128), b16),
             pltpu.VMEM((RMAX + 1, 2 * edge_rows, 128), b16),
@@ -390,18 +493,19 @@
             pltpu.VMEM((blocks, inner, CB, cols), b16),
             pltpu.VMEM((blocks, outer, CB, cols), b16),
             packed, packed, packed, packed,
+            far, far, far, far,
             edge, edge, edge, edge,
             pltpu.VMEM((chans + CB, 2 * chans), f32),
             pltpu.VMEM((peers, share, 2 * chans), f32),
             pltpu.VMEM((chans, 2 * chans), f32),
             pltpu.VMEM((8, 2 * chans), f32),
             pltpu.VMEM((peers, 8, 2 * chans), f32),
+            dma((2, blocks + early)), dma((2, blocks + early)),
             dma((2, blocks)), dma((2, blocks)), dma((2, blocks)), dma((2, blocks)),
-            dma((2, blocks)), dma((2, blocks)),
             dma((peers,)), dma((peers,)), dma((peers,)), dma((peers,)), dma((peers,)), dma((peers,)),
         ],
         compiler_params=pltpu.CompilerParams(
-            collective_id=0, has_side_effects=True, vmem_limit_bytes=32 * 1024 * 1024
+            collective_id=0, has_side_effects=True, vmem_limit_bytes=60 * 1024 * 1024
         ),
     )(radii, flat, valid)
     return (jnp.transpose(smoothed, (1, 0, 2)), mean.reshape(chans), cov)

time: 56.7 us -> 52.5 us (0.926)
  Pallas kernels: 50.1 us -> 46.9 us
  local copies, waits for them, and re-layouts: 5.79 us -> 4.72 us
    pallas_call x1, Pallas kernels: 50.1 us -> 46.9 us  [per_device(): pl.pallas_call(functools.partial(kernel, (n_ra, n_dec, rows, chans, cols)...]
    unnamed x9 -> x7, local copies, waits for them, and re-layouts: 5.79 us -> 4.72 us
where the time goes in v1:
time: 52.5 us; the launch traced here: 52.3 us
  Pallas kernels  46.9 us (89%)
  local copies, waits for them, and re-layouts  4.72 us (9%)
  between operations  0.66 us (1%)
    pallas_call x1, Pallas kernels, per_device(): pl.pallas_call(functools.partial(kernel, (n_ra, n_dec, rows, chans, cols)...  46.9 us
    unnamed x7, local copies, waits for them, and re-layouts  4.72 us

profile of v1, /device:TPU:0, one launch (start us, length us, event | category | flops | bytes accessed | tf_op | source)
XLA Modules:
  0.0 52.3 jit_solution(9466713937442987135)
XLA Ops:
  0.6 46.9 %shard_map.58 = (bf16[78,128,128]{2,1,0:T(8,128)(2,1)}, f32[1,128]{1,0:T(1,128)}, f32[256,128]{1,0:T(8,128)}) custom-call(s32[128]{0:T(128)} %radii_hbm.1, bf16[78,128,128]{2,1,0:T(8,128)(2,1)} %bitcast.3, s32[78,128]{1,0:T(8,128)} %valid_hbm.1), custom_call_target="tpu_custom_call" | custom-call | tf_op jit(solution)/shard_map/pallas_call | solution.py:469
  47.6 0.0 copy-start.1
  47.6 0.0 copy-start
  47.6 3.5 %copy.9 = bf16[128,78,128]{2,0,1:T(8,128)(2,1)} copy(bf16[128,78,128]{2,0,1:T(8,128)(2,1)} %bitcast.4) | data formatting | bytes 5111808
  51.2 0.0 copy-done.1
  51.2 0.5 copy.10
  51.7 0.0 copy-done
  51.7 0.7 %copy.11 = f32[256,128]{1,0:T(8,128)} copy(f32[256,128]{1,0:T(8,128)S(1)} %copy-done) | data formatting | bytes 262144
Async XLA Ops:
  47.6 3.6 %copy-start.1 = (f32[1,128]{1,0:T(1,128)S(1)}, f32[1,128]{1,0:T(1,128)}, u32[]{:S(2)}) copy-start(f32[1,128]{1,0:T(1,128)} %get-tuple-element.7) | copy-start | bytes 1540
  47.6 4.1 %copy-start = (f32[256,128]{1,0:T(8,128)S(1)}, f32[256,128]{1,0:T(8,128)}, u32[]{:S(2)}) copy-start(f32[256,128]{1,0:T(8,128)} %get-tuple-element.14) | copy-start | bytes 393220

commit v2 on v1

--- a/solution.py
+++ b/solution.py
@@ -446,6 +446,15 @@
     reducing(rank, lambda: each_peer(lambda p: ag(p, rank).wait_send()))
 
 
+def store(smoothed_ref, mean_ref, cov_ref, smoothed_hbm, mean_hbm, cov_hbm, sems):
+    pairs = ((smoothed_ref, smoothed_hbm), (mean_ref, mean_hbm), (cov_ref, cov_hbm))
+    copies = [pltpu.make_async_copy(src, dst, sems.at[i]) for i, (src, dst) in enumerate(pairs)]
+    for copy in copies:
+        copy.start()
+    for copy in copies:
+        copy.wait()
+
+
 def per_device(n_ra, n_dec, sky_maps, radii, valid):
     chans, rows, cols = sky_maps.shape
     blocks = chans // CB
@@ -462,16 +471,18 @@
     hbm = pl.BlockSpec(memory_space=pltpu.HBM)
     in_at, in_rows, edge_rows = inner_rows(rows)
     inner, outer = rows - 2 * RMAX, 2 * RMAX
-    flat = jnp.transpose(sky_maps, (1, 0, 2))
+    flat = pltpu.with_memory_space_constraint(jnp.transpose(sky_maps, (1, 0, 2)), pltpu.HBM)
+    radii = pltpu.with_memory_space_constraint(radii, pltpu.HBM)
+    valid = pltpu.with_memory_space_constraint(valid, pltpu.HBM)
     packed = pltpu.VMEM((blocks, per, CB, cols), b16)
     far = pltpu.VMEM((early, far_per, CB, cols), b16)
     edge = pltpu.VMEM((blocks, RMAX, CB, cols), b16)
     smoothed, mean, cov = pl.pallas_call(
         functools.partial(kernel, (n_ra, n_dec, rows, chans, cols)),
         out_shape=(
-            jax.ShapeDtypeStruct((rows, chans, cols), b16),
-            jax.ShapeDtypeStruct((1, chans), f32),
-            jax.ShapeDtypeStruct((2 * chans, chans), f32),
+            pltpu.VMEM((rows, chans, cols), b16),
+            pltpu.VMEM((1, chans), f32),
+            pltpu.VMEM((2 * chans, chans), f32),
         ),
         in_specs=[hbm, hbm, hbm],
         out_specs=(vmem, vmem, vmem),
@@ -505,9 +516,20 @@
             dma((peers,)), dma((peers,)), dma((peers,)), dma((peers,)), dma((peers,)), dma((peers,)),
         ],
         compiler_params=pltpu.CompilerParams(
-            collective_id=0, has_side_effects=True, vmem_limit_bytes=60 * 1024 * 1024
+            collective_id=0, has_side_effects=True, vmem_limit_bytes=40 * 1024 * 1024
         ),
     )(radii, flat, valid)
+    smoothed, mean, cov = pl.pallas_call(
+        store,
+        out_shape=(
+            jax.ShapeDtypeStruct((rows, chans, cols), b16),
+            jax.ShapeDtypeStruct((1, chans), f32),
+            jax.ShapeDtypeStruct((2 * chans, chans), f32),
+        ),
+        in_specs=(vmem, vmem, vmem),
+        out_specs=(hbm, hbm, hbm),
+        scratch_shapes=[dma((3,))],
+    )(*(pltpu.with_memory_space_constraint(part, pltpu.VMEM) for part in (smoothed, mean, cov)))
     return (jnp.transpose(smoothed, (1, 0, 2)), mean.reshape(chans), cov)
 
 

time: 52.5 us -> 47.7 us (0.909)
  local copies, waits for them, and re-layouts: 4.72 us -> 0 us
    unnamed x7 -> x0, local copies, waits for them, and re-layouts: 4.72 us -> none
    pallas_call x1, Pallas kernels: 46.9 us -> 45.4 us  [per_device(): pl.pallas_call(functools.partial(kernel, (n_ra, n_dec, rows, chans, cols)...]
    pallas_call x0 -> x1, Pallas kernels: none -> 1.53 us  [per_device(): pl.pallas_call(store, out_shape=(jax.ShapeDtypeStruct((rows, chans, cols)...]
where the time goes in v2:
time: 47.7 us; the launch traced here: 47.6 us
  Pallas kernels  46.9 us (98%)
  between operations  0.64 us (1%)
    pallas_call x1, Pallas kernels, per_device(): pl.pallas_call(functools.partial(kernel, (n_ra, n_dec, rows, chans, cols)...  45.4 us
    pallas_call x1, Pallas kernels, per_device(): pl.pallas_call(store, out_shape=(jax.ShapeDtypeStruct((rows, chans, cols)...  1.53 us

profile of v2, /device:TPU:0, one launch (start us, length us, event | category | flops | bytes accessed | tf_op | source)
XLA Modules:
  0.0 47.6 jit_solution(5426499216315422179)
XLA Ops:
  0.6 45.4 %shard_map.58 = (bf16[78,128,128]{2,1,0:T(8,128)(2,1)S(1)}, f32[1,128]{1,0:T(1,128)S(1)}, f32[256,128]{1,0:T(8,128)S(1)}) custom-call(s32[128]{0:T(128)} %radii_hbm.1, bf16[78,128,128]{2,1,0:T(8,128)(2,1)} %bitcast.3, s32[78,128]{1,0:T(8,128)} %valid_hbm.1), custom_call_target="tpu_custom_call" | custom-call | tf_op jit(solution)/shard_map/pallas_call | solution.py:480
  46.1 1.5 %shard_map.59 = (bf16[78,128,128]{2,1,0:T(8,128)(2,1)}, f32[1,128]{1,0:T(1,128)}, f32[256,128]{1,0:T(8,128)}) custom-call(bf16[78,128,128]{2,1,0:T(8,128)(2,1)S(1)} %get-tuple-element.9.smoothed_ref, f32[1,128]{1,0:T(1,128)S(1)} %get-tuple-element.10.mean_ref, f32[256,128]{1,0:T(8,128)S(1)} %get-tuple-element.11.cov_ref), custom_call_target="tpu_custom_call" | custom-call | tf_op jit(solution)/shard_map/pallas_call | solution.py:522

commit v3 on v2

--- a/solution.py
+++ b/solution.py
@@ -11,6 +11,8 @@
 WIDE = RMAX + 1
 CB = 16
 EARLY = 2
+SINGLE = 2
+TABLES_LESS = 6
 MESH = pl.DeviceIdType.MESH
 
 
@@ -37,6 +39,7 @@
     sky_ref, valid_ref, radii_ref, loads,
     tab_dec, tab_in, tab_ed, xs, hs, os, ps, vb, mine_in, mine_ed, other_in, other_ed,
     pack_up, pack_dn, halo_lo, halo_hi, far_up, far_dn, far_lo, far_hi, edge_lo, edge_hi, z_before, z_after,
+    raw_before, raw_after,
     acc, shares, total, aux, aux_all,
     s_dec, r_dec, s_ra, r_ra, s_band, r_band, s_rs, r_rs, s_ag, r_ag, s_aux, r_aux,
 ):
@@ -61,6 +64,11 @@
         return {"ra": p // n_dec, "dec": lax.rem(p, n_dec)}
 
     def each_peer(body):
+        if peers <= 8:
+            for d in range(1, peers):
+                body(lax.rem(rank + d, peers))
+            return
+
         def step(d, carry):
             body(lax.rem(rank + d, peers))
             return carry
@@ -100,10 +108,6 @@
             return carry
         lax.fori_loop(first, last, step, 0)
 
-    for_blocks(lambda b: load_sky(b).start())
-    load_valid.start()
-    load_radii.start()
-    pl.semaphore_wait(barrier, peers)
 
     def remote(src, dst, send, recv, target):
         return pltpu.make_async_remote_copy(
@@ -126,19 +130,25 @@
             far_dn.at[j], far_hi.at[j], s_dec.at[1, blocks + j], r_dec.at[1, blocks + j], {"dec": dec - 1}
         )
 
-    def sky_up(b):
-        rim = sky_hbm.at[pl.ds(rows - RMAX, RMAX), pl.ds(pl.multiple_of(b * CB, CB), CB), :]
-        return remote(rim, z_before.at[b], s_ra.at[0, b], r_ra.at[0, b], {"ra": nxt})
-
-    def sky_dn(b):
-        rim = sky_hbm.at[pl.ds(0, RMAX), pl.ds(pl.multiple_of(b * CB, CB), CB), :]
-        return remote(rim, z_after.at[b], s_ra.at[1, b], r_ra.at[1, b], {"ra": prv})
-
-    def ra_up(b):
-        return remote(edge_hi.at[b], z_before.at[b], s_ra.at[0, b], r_ra.at[0, b], {"ra": nxt})
-
-    def ra_dn(b):
-        return remote(edge_lo.at[b], z_after.at[b], s_ra.at[1, b], r_ra.at[1, b], {"ra": prv})
+    def sky_up():
+        rim = sky_hbm.at[pl.ds(rows - RMAX, RMAX), pl.ds(late * CB, chans - late * CB), :]
+        return remote(rim, raw_before, s_ra.at[0, late], r_ra.at[0, late], {"ra": nxt})
+
+    def sky_dn():
+        rim = sky_hbm.at[pl.ds(0, RMAX), pl.ds(late * CB, chans - late * CB), :]
+        return remote(rim, raw_after, s_ra.at[1, late], r_ra.at[1, late], {"ra": prv})
+
+    def ra_up(b, n):
+        part = pl.ds(b, n)
+        return remote(edge_hi.at[part], z_before.at[part], s_ra.at[0, b], r_ra.at[0, b], {"ra": nxt})
+
+    def ra_dn(b, n):
+        part = pl.ds(b, n)
+        return remote(edge_lo.at[part], z_after.at[part], s_ra.at[1, b], r_ra.at[1, b], {"ra": prv})
+
+    def ra_both(b, n, body):
+        body(ra_up(b, n))
+        body(ra_dn(b, n))
 
     def to_twin(k, b):
         mine, other = ((mine_ed, other_ed), (mine_in, other_in))[k]
@@ -149,11 +159,16 @@
     inner = rows - 2 * RMAX
     order = [*range(RMAX), *range(rows - RMAX, rows), *range(RMAX, rows - RMAX)]
 
-    def send_sky(b):
-        sky_up(b).start()
-        sky_dn(b).start()
-
-    for_blocks(send_sky, late)
+    def send_rims():
+        @pl.when(ra == 0)
+        def _():
+            sky_dn().start()
+            sky_up().start()
+
+        @pl.when(ra > 0)
+        def _():
+            sky_up().start()
+            sky_dn().start()
 
     def load_block(b):
         at = pl.multiple_of(b * CB, CB)
@@ -174,6 +189,14 @@
         return result.astype(jnp.bfloat16)
 
     def pack_block(b):
+        pack_only(b)
+        send_packed(b)
+
+    def send_packed(b):
+        pl.when(has_hi)(lambda: dec_up(b).start())
+        pl.when(has_lo)(lambda: dec_dn(b).start())
+
+    def pack_only(b):
         load_sky(b).wait()
         at = pl.multiple_of(b * CB, CB)
 
@@ -183,24 +206,20 @@
         @pl.when(has_hi)
         def _():
             pack_up[b] = packed(read, rows, per, cols - WIDE)
-            dec_up(b).start()
 
         @pl.when(has_lo)
         def _():
             pack_dn[b] = packed(read, rows, per, 0)
-            dec_dn(b).start()
 
     def pack_far(j):
-        b = late + j
-        sky_up(b).wait_recv()
-        sky_dn(b).wait_recv()
+        here = pl.ds(pl.multiple_of(j * CB, CB), CB)
 
         def read(first, last):
             both = []
             if first < RMAX:
-                both.append(z_before[b, first:min(last, RMAX)])
+                both.append(raw_before[first:min(last, RMAX), here, :])
             if last > RMAX:
-                both.append(z_after[b, max(first, RMAX) - RMAX:last - RMAX])
+                both.append(raw_after[max(first, RMAX) - RMAX:last - RMAX, here, :])
             return jnp.concatenate(both, axis=0)
 
         @pl.when(has_hi)
@@ -214,10 +233,30 @@
             far_dec_dn(j).start()
 
     ahead = min(2, blocks)
-    for b in range(ahead):
-        pack_block(jnp.int32(b))
-
-    lax.fori_loop(1, RMAX + 1, table, 0)
+    is_last = ra == n_ra - 1
+    ready = jnp.maximum(RMAX + 1 - TABLES_LESS * ra, 1)
+
+    def start_loads():
+        for_blocks(lambda b: load_sky(b).start())
+        load_valid.start()
+        load_radii.start()
+
+    @pl.when(jnp.logical_not(is_last))
+    def _():
+        start_loads()
+        for_blocks(pack_only, 0, ahead)
+
+    lax.fori_loop(1, ready, table, 0)
+    pl.semaphore_wait(barrier, peers)
+    send_rims()
+
+    @pl.when(is_last)
+    def _():
+        start_loads()
+        for_blocks(pack_only, 0, ahead)
+
+    for_blocks(send_packed, 0, ahead)
+    lax.fori_loop(ready, RMAX + 1, table, 0)
     spare = xs.shape[0] - rows * CB
     xs[rows * CB:, :] = jnp.zeros((spare, cols), jnp.float32)
     if n_dec == 1:
@@ -225,6 +264,7 @@
     load_radii.wait()
     load_valid.wait()
     weights = valid_ref[...].astype(jnp.float32)
+    aux[...] = jnp.broadcast_to(jnp.sum(weights, keepdims=True), (8, chans))
     for at, x in enumerate(order):
         vb[at] = jnp.broadcast_to(weights[x:x + 1, :], (CB, cols)).astype(jnp.bfloat16)
 
@@ -267,7 +307,7 @@
                 tab[rr], column, preferred_element_type=jnp.float32
             )
 
-    def gram_of(mine, other, first, height):
+    def gram_of(mine, other, first, height, half=None):
         steps = next(n for n in (8, 6, 4, 2, 1) if height % n == 0)
         if height % 34 == 0:
             steps = 34
@@ -279,15 +319,35 @@
                 return ref[:, pl.ds(x, 1), :, :].reshape(chans, cols)
 
             own = jnp.concatenate([row(mine, i * steps + s) for s in range(steps)], axis=1)
-            oth = jnp.concatenate([row(other, i * steps + s) for s in range(steps)], axis=1)
+            if half != 0:
+                oth = jnp.concatenate([row(other, i * steps + s) for s in range(steps)], axis=1)
             msk = jnp.concatenate([vb[first + i * steps + s] for s in range(steps)], axis=1)
-            acc[...] += lax.dot_general(
-                jnp.concatenate([own, msk], axis=0), jnp.concatenate([own, oth], axis=0),
+            if half is None:
+                across = jnp.concatenate([own, oth], axis=0)
+            else:
+                across = oth if half else own
+            product = lax.dot_general(
+                jnp.concatenate([own, msk], axis=0), across,
                 (((1,), (1,)), ((), ())), preferred_element_type=jnp.float32,
             )
+            if half is None:
+                acc[0] += product[:, 0:chans]
+                acc[1] += product[:, chans:2 * chans]
+            else:
+                acc[half] += product
             return carry
 
         lax.fori_loop(0, height // steps, gram, 0)
+
+    paired = 2 * max((late - SINGLE) // 2, 0)
+
+    def send_edges(b):
+        pl.when((b < paired) & (lax.rem(b, 2) == 1))(lambda: ra_both(b - 1, 2, lambda c: c.start()))
+        pl.when(b >= paired)(lambda: ra_both(b, 1, lambda c: c.start()))
+
+    def for_edges(b, body):
+        pl.when((b < paired) & (lax.rem(b, 2) == 0))(lambda: ra_both(b, 2, body))
+        pl.when(b >= paired)(lambda: ra_both(b, 1, body))
 
     def dec_block(b, carry):
         @pl.when(b + ahead < blocks)
@@ -311,8 +371,7 @@
             edge_lo[b] = ps[b, 0:RMAX * CB, :].reshape(RMAX, CB, cols).astype(jnp.bfloat16)
             last = ps[b, (rows - RMAX) * CB:rows * CB, :]
             edge_hi[b] = last.reshape(RMAX, CB, cols).astype(jnp.bfloat16)
-            ra_up(b).start()
-            ra_dn(b).start()
+            send_edges(b)
 
         smooth_rows(b, tab_in, in_rows)
         at = RMAX - in_at
@@ -320,15 +379,21 @@
         out_ref[RMAX:rows - RMAX, pl.ds(pl.multiple_of(b * CB, CB), CB), :] = smooth
         mine_in[b] = smooth * vb[2 * RMAX:rows]
         to_twin(1, b).start()
-        pl.when(b == late // 2)(lambda: for_blocks(pack_far, 0, blocks - late))
+        @pl.when(b == late // 2)
+        def _():
+            sky_up().wait_recv()
+            sky_dn().wait_recv()
+            for_blocks(pack_far, 0, blocks - late)
+
         return carry
 
     lax.fori_loop(0, blocks, dec_block, 0)
 
     def far_block(j):
         b = late + j
-        for first, ref in ((0, z_before), (RMAX, z_after)):
-            rim = ref[b].astype(jnp.float32)
+        here = pl.ds(pl.multiple_of(j * CB, CB), CB)
+        for first, ref in ((0, raw_before), (RMAX, raw_after)):
+            rim = ref[:, here, :].astype(jnp.float32)
             xs[first * CB:(first + RMAX) * CB, :] = rim.reshape(RMAX * CB, cols)
         pl.when(has_lo)(lambda: far_dec_up(j).wait_recv())
         pl.when(has_hi)(lambda: far_dec_dn(j).wait_recv())
@@ -352,8 +417,7 @@
 
         @pl.when(b < late)
         def _():
-            ra_up(b).wait_recv()
-            ra_dn(b).wait_recv()
+            for_edges(b, lambda c: c.wait_recv())
             before = z_before[b].astype(jnp.float32)
             ps[b, (ext - RMAX) * CB:ext * CB, :] = before.reshape(RMAX * CB, cols)
             after = z_after[b].astype(jnp.float32)
@@ -372,20 +436,17 @@
         return carry
 
     lax.fori_loop(0, blocks, ra_block, 0)
-    for_blocks(lambda b: to_twin(0, b).wait_recv())
-    gram_of(mine_ed, other_ed, 0, 2 * RMAX)
-    count = jnp.sum(weights, keepdims=True)
-    aux[...] = jnp.where(iota((8, 2 * chans), 0) == 0, acc[chans:chans + 8, :], count)
-
     def part_of(p):
-        return acc.at[pl.ds(pl.multiple_of(p * share, share), share), :]
-
-    def rs(p, slot):
-        return remote(part_of(p), shares.at[slot], s_rs.at[p], r_rs.at[slot], peer_id(p))
-
-    def ag(p, slot):
-        mypart = total.at[pl.ds(pl.multiple_of(slot * share, share), share), :]
-        return remote(mypart, mypart, s_ag.at[p], r_ag.at[slot], peer_id(p))
+        return pl.ds(pl.multiple_of(p * share, share), share)
+
+    def rs(k, p, slot):
+        return remote(
+            acc.at[k, part_of(p)], shares.at[k, slot], s_rs.at[k, p], r_rs.at[k, slot], peer_id(p)
+        )
+
+    def ag(k, p, slot):
+        mine = total.at[k, part_of(slot)]
+        return remote(mine, mine, s_ag.at[k, p], r_ag.at[k, slot], peer_id(p))
 
     def au(p, slot):
         return remote(aux, aux_all.at[slot], s_aux.at[p], r_aux.at[slot], peer_id(p))
@@ -396,31 +457,16 @@
         else:
             pl.when(p < reducers)(body)
 
-    each_peer(lambda p: reducing(p, lambda: rs(p, rank).start()))
+    gram_of(mine_ed, other_ed, 0, 2 * RMAX, 0)
+    each_peer(lambda p: reducing(p, lambda: rs(0, p, rank).start()))
+    for_blocks(lambda b: to_twin(0, b).wait_recv())
+    gram_of(mine_ed, other_ed, 0, 2 * RMAX, 1)
+    each_peer(lambda p: reducing(p, lambda: rs(1, p, rank).start()))
+    place = iota((8, chans), 0)
+    for k in range(2):
+        aux[...] = jnp.where(place == k, acc[k, chans:chans + 8, :], aux[...])
     each_peer(lambda p: au(p, rank).start())
     aux_all[rank] = aux[...]
-
-    def reduce_own():
-        shares[rank] = acc[pl.ds(pl.multiple_of(rank * share, share), share), :]
-        each_peer(lambda p: rs(rank, p).wait_recv())
-        whole = shares[0]
-        whole = lax.fori_loop(1, peers, lambda p, t: t + shares[p], whole)
-        total[pl.ds(pl.multiple_of(rank * share, share), share), :] = whole
-        each_peer(lambda p: ag(p, rank).start())
-
-    reducing(rank, reduce_own)
-    each_peer(lambda p: au(p, p).wait_recv())
-    sums = lax.fori_loop(1, peers, lambda p, t: t + aux_all[p], aux_all[0])
-    count = sums[1:2, 0:1]
-    means = sums[0:1, :] / count
-    mean_ref[...] = means[:, 0:chans]
-    column = jnp.transpose(jnp.broadcast_to(means[:, 0:chans], (chans, chans)))
-    each_peer(lambda p: reducing(p, lambda: ag(p, p).wait_recv()))
-    for k in range(2):
-        across = means[:, k * chans:(k + 1) * chans]
-        block = (total[:, k * chans:(k + 1) * chans] - count * column * across) / (count - 1.0)
-        place = band if k == 0 else 1 - band
-        cov_ref[pl.ds(pl.multiple_of(place * chans, chans), chans), :] = jnp.transpose(block)
 
     def finish(b):
         pl.when(has_hi)(lambda: dec_up(b).wait_send())
@@ -429,21 +475,43 @@
         to_twin(1, b).wait_send()
 
     def finish_late(b):
-        ra_up(b).wait_send()
-        ra_dn(b).wait_send()
+        for_edges(b, lambda c: c.wait_send())
 
     def finish_early(j):
-        sky_up(late + j).wait_send()
-        sky_dn(late + j).wait_send()
         pl.when(has_hi)(lambda: far_dec_up(j).wait_send())
         pl.when(has_lo)(lambda: far_dec_dn(j).wait_send())
 
     for_blocks(finish)
     for_blocks(finish_late, 0, late)
     for_blocks(finish_early, 0, blocks - late)
-    each_peer(lambda p: reducing(p, lambda: rs(p, rank).wait_send()))
+    sky_up().wait_send()
+    sky_dn().wait_send()
+    def reduce_own(k):
+        shares[k, rank] = acc[k, part_of(rank), :]
+        each_peer(lambda p: rs(k, rank, p).wait_recv())
+        whole = shares[k, 0]
+        whole = lax.fori_loop(1, peers, lambda p, t: t + shares[k, p], whole)
+        total[k, part_of(rank), :] = whole
+        each_peer(lambda p: ag(k, p, rank).start())
+
+    for k in range(2):
+        reducing(rank, functools.partial(reduce_own, k))
+    each_peer(lambda p: au(p, p).wait_recv())
+    sums = lax.fori_loop(1, peers, lambda p, t: t + aux_all[p], aux_all[0])
+    count = sums[2:3, 0:1]
+    means = sums / count
+    mean_ref[...] = means[0:1, :]
+    column = jnp.transpose(jnp.broadcast_to(means[0:1, :], (chans, chans)))
+    for k in range(2):
+        each_peer(lambda p: reducing(p, lambda: ag(k, p, p).wait_recv()))
+        block = (total[k] - count * column * means[k:k + 1, :]) / (count - 1.0)
+        place = band if k == 0 else 1 - band
+        cov_ref[pl.ds(pl.multiple_of(place * chans, chans), chans), :] = jnp.transpose(block)
+
+    for k in range(2):
+        each_peer(lambda p: reducing(p, lambda: rs(k, p, rank).wait_send()))
+        reducing(rank, lambda: each_peer(lambda p: ag(k, p, rank).wait_send()))
     each_peer(lambda p: au(p, rank).wait_send())
-    reducing(rank, lambda: each_peer(lambda p: ag(p, rank).wait_send()))
 
 
 def store(smoothed_ref, mean_ref, cov_ref, smoothed_hbm, mean_hbm, cov_hbm, sems):
@@ -476,7 +544,8 @@
     valid = pltpu.with_memory_space_constraint(valid, pltpu.HBM)
     packed = pltpu.VMEM((blocks, per, CB, cols), b16)
     far = pltpu.VMEM((early, far_per, CB, cols), b16)
-    edge = pltpu.VMEM((blocks, RMAX, CB, cols), b16)
+    raw = pltpu.VMEM((RMAX, early * CB, cols), b16)
+    edge = pltpu.VMEM((blocks - early, RMAX, CB, cols), b16)
     smoothed, mean, cov = pl.pallas_call(
         functools.partial(kernel, (n_ra, n_dec, rows, chans, cols)),
         out_shape=(
@@ -505,15 +574,15 @@
             pltpu.VMEM((blocks, outer, CB, cols), b16),
             packed, packed, packed, packed,
             far, far, far, far,
-            edge, edge, edge, edge,
-            pltpu.VMEM((chans + CB, 2 * chans), f32),
-            pltpu.VMEM((peers, share, 2 * chans), f32),
-            pltpu.VMEM((chans, 2 * chans), f32),
-            pltpu.VMEM((8, 2 * chans), f32),
-            pltpu.VMEM((peers, 8, 2 * chans), f32),
+            edge, edge, edge, edge, raw, raw,
+            pltpu.VMEM((2, chans + CB, chans), f32),
+            pltpu.VMEM((2, peers, share, chans), f32),
+            pltpu.VMEM((2, chans, chans), f32),
+            pltpu.VMEM((8, chans), f32),
+            pltpu.VMEM((peers, 8, chans), f32),
             dma((2, blocks + early)), dma((2, blocks + early)),
             dma((2, blocks)), dma((2, blocks)), dma((2, blocks)), dma((2, blocks)),
-            dma((peers,)), dma((peers,)), dma((peers,)), dma((peers,)), dma((peers,)), dma((peers,)),
+            dma((2, peers)), dma((2, peers)), dma((2, peers)), dma((2, peers)), dma((peers,)), dma((peers,)),
         ],
         compiler_params=pltpu.CompilerParams(
             collective_id=0, has_side_effects=True, vmem_limit_bytes=40 * 1024 * 1024

time: 47.7 us -> 46.9 us (0.983)
  Pallas kernels: 46.9 us -> 46.1 us
    pallas_call x1, Pallas kernels: 45.4 us -> 44.6 us  [per_device(): pl.pallas_call(functools.partial(kernel, (n_ra, n_dec, rows, chans, cols)...]
where the time goes in v3:
time: 46.9 us; the launch traced here: 46.7 us
  Pallas kernels  46.1 us (98%)
  between operations  0.64 us (1%)
    pallas_call x1, Pallas kernels, per_device(): pl.pallas_call(functools.partial(kernel, (n_ra, n_dec, rows, chans, cols)...  44.6 us
    pallas_call x1, Pallas kernels, per_device(): pl.pallas_call(store, out_shape=(jax.ShapeDtypeStruct((rows, chans, cols)...  1.53 us

profile of v3, /device:TPU:0, one launch (start us, length us, event | category | flops | bytes accessed | tf_op | source)
XLA Modules:
  0.0 46.7 jit_solution(15395535813633390377)
XLA Ops:
  0.6 44.6 %shard_map.58 = (bf16[78,128,128]{2,1,0:T(8,128)(2,1)S(1)}, f32[1,128]{1,0:T(1,128)S(1)}, f32[256,128]{1,0:T(8,128)S(1)}) custom-call(s32[128]{0:T(128)} %radii_hbm.1, bf16[78,128,128]{2,1,0:T(8,128)(2,1)} %bitcast.3, s32[78,128]{1,0:T(8,128)} %valid_hbm.1), custom_call_target="tpu_custom_call" | custom-call | tf_op jit(solution)/shard_map/pallas_call | solution.py:549
  45.2 1.5 %shard_map.59 = (bf16[78,128,128]{2,1,0:T(8,128)(2,1)}, f32[1,128]{1,0:T(1,128)}, f32[256,128]{1,0:T(8,128)}) custom-call(bf16[78,128,128]{2,1,0:T(8,128)(2,1)S(1)} %get-tuple-element.9.smoothed_ref, f32[1,128]{1,0:T(1,128)S(1)} %get-tuple-element.10.mean_ref, f32[256,128]{1,0:T(8,128)S(1)} %get-tuple-element.11.cov_ref), custom_call_target="tpu_custom_call" | custom-call | tf_op jit(solution)/shard_map/pallas_call | solution.py:591

commit v4 on v3

--- a/solution.py
+++ b/solution.py
@@ -40,7 +40,7 @@
     tab_dec, tab_in, tab_ed, xs, hs, os, ps, vb, mine_in, mine_ed, other_in, other_ed,
     pack_up, pack_dn, halo_lo, halo_hi, far_up, far_dn, far_lo, far_hi, edge_lo, edge_hi, z_before, z_after,
     raw_before, raw_after,
-    acc, shares, total, aux, aux_all,
+    acc, shares, total, ended, column, aux, aux_all,
     s_dec, r_dec, s_ra, r_ra, s_band, r_band, s_rs, r_rs, s_ag, r_ag, s_aux, r_aux,
 ):
     n_ra, n_dec, rows, chans, cols = dims
@@ -51,7 +51,7 @@
     far_per = -(-2 * RMAX // groups)
     late = blocks - early_blocks(blocks)
     peers = n_ra * n_dec
-    reducers = min(peers, chans // 8)
+    reducers = min(peers, chans // 16)
     share = chans // reducers
     ext = 128
     in_at, in_rows, edge_rows = inner_rows(rows)
@@ -73,6 +73,17 @@
             body(lax.rem(rank + d, peers))
             return carry
         lax.fori_loop(1, peers, step, 0)
+
+    def in_order(body):
+        def step(p, carry):
+            pl.when(p != rank)(lambda: body(p))
+            return carry
+
+        if peers <= 8:
+            for p in range(peers):
+                step(p, 0)
+        else:
+            lax.fori_loop(0, peers, step, 0)
 
     def table(r, carry):
         radius = r.astype(jnp.float32)
@@ -445,7 +456,7 @@
         )
 
     def ag(k, p, slot):
-        mine = total.at[k, part_of(slot)]
+        mine = (total, ended)[k].at[part_of(slot)]
         return remote(mine, mine, s_ag.at[k, p], r_ag.at[k, slot], peer_id(p))
 
     def au(p, slot):
@@ -461,11 +472,11 @@
     each_peer(lambda p: reducing(p, lambda: rs(0, p, rank).start()))
     for_blocks(lambda b: to_twin(0, b).wait_recv())
     gram_of(mine_ed, other_ed, 0, 2 * RMAX, 1)
-    each_peer(lambda p: reducing(p, lambda: rs(1, p, rank).start()))
     place = iota((8, chans), 0)
     for k in range(2):
         aux[...] = jnp.where(place == k, acc[k, chans:chans + 8, :], aux[...])
     each_peer(lambda p: au(p, rank).start())
+    each_peer(lambda p: reducing(p, lambda: rs(1, p, rank).start()))
     aux_all[rank] = aux[...]
 
     def finish(b):
@@ -486,32 +497,42 @@
     for_blocks(finish_early, 0, blocks - late)
     sky_up().wait_send()
     sky_dn().wait_send()
-    def reduce_own(k):
+    def whole_of(k):
         shares[k, rank] = acc[k, part_of(rank), :]
         each_peer(lambda p: rs(k, rank, p).wait_recv())
-        whole = shares[k, 0]
-        whole = lax.fori_loop(1, peers, lambda p, t: t + shares[k, p], whole)
-        total[k, part_of(rank), :] = whole
-        each_peer(lambda p: ag(k, p, rank).start())
-
-    for k in range(2):
-        reducing(rank, functools.partial(reduce_own, k))
+        return lax.fori_loop(1, peers, lambda p, t: t + shares[k, p], shares[k, 0])
+
+    def reduce_first():
+        total[part_of(rank), :] = whole_of(0)
+        in_order(lambda p: ag(0, p, rank).start())
+
+    reducing(rank, reduce_first)
     each_peer(lambda p: au(p, p).wait_recv())
     sums = lax.fori_loop(1, peers, lambda p, t: t + aux_all[p], aux_all[0])
     count = sums[2:3, 0:1]
     means = sums / count
     mean_ref[...] = means[0:1, :]
-    column = jnp.transpose(jnp.broadcast_to(means[0:1, :], (chans, chans)))
+    column[...] = jnp.transpose(jnp.broadcast_to(means[0:1, :], (chans, chans)))
+
+    def reduce_second():
+        block = whole_of(1) - count * column[part_of(rank), :] * means[1:2, :]
+        ended[part_of(rank), :] = (block / (count - 1.0)).astype(jnp.bfloat16)
+        in_order(lambda p: ag(1, p, rank).start())
+
+    reducing(rank, reduce_second)
+    each_peer(lambda p: au(p, rank).wait_send())
+    for k in range(2):
+        each_peer(lambda p: reducing(p, lambda: rs(k, p, rank).wait_send()))
     for k in range(2):
         each_peer(lambda p: reducing(p, lambda: ag(k, p, p).wait_recv()))
-        block = (total[k] - count * column * means[k:k + 1, :]) / (count - 1.0)
         place = band if k == 0 else 1 - band
+        if k == 0:
+            block = (total[...] - count * column[...] * means[0:1, :]) / (count - 1.0)
+        else:
+            block = ended[...].astype(jnp.float32)
         cov_ref[pl.ds(pl.multiple_of(place * chans, chans), chans), :] = jnp.transpose(block)
-
     for k in range(2):
-        each_peer(lambda p: reducing(p, lambda: rs(k, p, rank).wait_send()))
         reducing(rank, lambda: each_peer(lambda p: ag(k, p, rank).wait_send()))
-    each_peer(lambda p: au(p, rank).wait_send())
 
 
 def store(smoothed_ref, mean_ref, cov_ref, smoothed_hbm, mean_hbm, cov_hbm, sems):
@@ -530,7 +551,7 @@
     groups = cols // WIDE
     per = -(-rows // groups)
     peers = n_ra * n_dec
-    share = chans // min(peers, chans // 8)
+    share = chans // min(peers, chans // 16)
     early = early_blocks(blocks)
     far_per = -(-2 * RMAX // groups)
     tall = max(per * groups, rows8)
@@ -577,7 +598,9 @@
             edge, edge, edge, edge, raw, raw,
             pltpu.VMEM((2, chans + CB, chans), f32),
             pltpu.VMEM((2, peers, share, chans), f32),
-            pltpu.VMEM((2, chans, chans), f32),
+            pltpu.VMEM((chans, chans), f32),
+            pltpu.VMEM((chans, chans), b16),
+            pltpu.VMEM((chans, chans), f32),
             pltpu.VMEM((8, chans), f32),
             pltpu.VMEM((peers, 8, chans), f32),
             dma((2, blocks + early)), dma((2, blocks + early)),

time: 46.9 us -> 46.8 us (level)
  no operation moved by 1% of the time
where the time goes in v4:
time: 46.8 us; the launch traced here: 46.7 us
  Pallas kernels  46.1 us (99%)
  between operations  0.64 us (1%)
    pallas_call x1, Pallas kernels, per_device(): pl.pallas_call(functools.partial(kernel, (n_ra, n_dec, rows, chans, cols)...  44.5 us
    pallas_call x1, Pallas kernels, per_device(): pl.pallas_call(store, out_shape=(jax.ShapeDtypeStruct((rows, chans, cols)...  1.53 us

profile of v4, /device:TPU:0, one launch (start us, length us, event | category | flops | bytes accessed | tf_op | source)
XLA Modules:
  0.0 46.7 jit_solution(10539926521852699396)
XLA Ops:
  0.6 44.5 %shard_map.58 = (bf16[78,128,128]{2,1,0:T(8,128)(2,1)S(1)}, f32[1,128]{1,0:T(1,128)S(1)}, f32[256,128]{1,0:T(8,128)S(1)}) custom-call(s32[128]{0:T(128)} %radii_hbm.1, bf16[78,128,128]{2,1,0:T(8,128)(2,1)} %bitcast.3, s32[78,128]{1,0:T(8,128)} %valid_hbm.1), custom_call_target="tpu_custom_call" | custom-call | tf_op jit(solution)/shard_map/pallas_call | solution.py:570
  45.2 1.5 %shard_map.59 = (bf16[78,128,128]{2,1,0:T(8,128)(2,1)}, f32[1,128]{1,0:T(1,128)}, f32[256,128]{1,0:T(8,128)}) custom-call(bf16[78,128,128]{2,1,0:T(8,128)(2,1)S(1)} %get-tuple-element.9.smoothed_ref, f32[1,128]{1,0:T(1,128)S(1)} %get-tuple-element.10.mean_ref, f32[256,128]{1,0:T(8,128)S(1)} %get-tuple-element.11.cov_ref), custom_call_target="tpu_custom_call" | custom-call | tf_op jit(solution)/shard_map/pallas_call | solution.py:614

commit v5 on v3

--- a/solution.py
+++ b/solution.py
@@ -74,6 +74,17 @@
             return carry
         lax.fori_loop(1, peers, step, 0)
 
+    def in_order(body):
+        def step(p, carry):
+            pl.when(p != rank)(lambda: body(p))
+            return carry
+
+        if peers <= 8:
+            for p in range(peers):
+                step(p, 0)
+        else:
+            lax.fori_loop(0, peers, step, 0)
+
     def table(r, carry):
         radius = r.astype(jnp.float32)
         spread = 0.5 * radius
@@ -492,11 +503,14 @@
         whole = shares[k, 0]
         whole = lax.fori_loop(1, peers, lambda p, t: t + shares[k, p], whole)
         total[k, part_of(rank), :] = whole
-        each_peer(lambda p: ag(k, p, rank).start())
+        in_order(lambda p: ag(k, p, rank).start())
 
     for k in range(2):
         reducing(rank, functools.partial(reduce_own, k))
     each_peer(lambda p: au(p, p).wait_recv())
+    each_peer(lambda p: au(p, rank).wait_send())
+    for k in range(2):
+        each_peer(lambda p: reducing(p, lambda: rs(k, p, rank).wait_send()))
     sums = lax.fori_loop(1, peers, lambda p, t: t + aux_all[p], aux_all[0])
     count = sums[2:3, 0:1]
     means = sums / count
@@ -509,9 +523,7 @@
         cov_ref[pl.ds(pl.multiple_of(place * chans, chans), chans), :] = jnp.transpose(block)
 
     for k in range(2):
-        each_peer(lambda p: reducing(p, lambda: rs(k, p, rank).wait_send()))
         reducing(rank, lambda: each_peer(lambda p: ag(k, p, rank).wait_send()))
-    each_peer(lambda p: au(p, rank).wait_send())
 
 
 def store(smoothed_ref, mean_ref, cov_ref, smoothed_hbm, mean_hbm, cov_hbm, sems):

time: 46.9 us -> 46.8 us (level)
  no operation moved by 1% of the time
where the time goes in v5:
time: 46.8 us; the launch traced here: 46.7 us
  Pallas kernels  46 us (98%)
  between operations  0.64 us (1%)
    pallas_call x1, Pallas kernels, per_device(): pl.pallas_call(functools.partial(kernel, (n_ra, n_dec, rows, chans, cols)...  44.5 us
    pallas_call x1, Pallas kernels, per_device(): pl.pallas_call(store, out_shape=(jax.ShapeDtypeStruct((rows, chans, cols)...  1.53 us

profile of v5, /device:TPU:0, one launch (start us, length us, event | category | flops | bytes accessed | tf_op | source)
XLA Modules:
  0.0 46.7 jit_solution(478523532805797895)
XLA Ops:
  0.6 44.5 %shard_map.58 = (bf16[78,128,128]{2,1,0:T(8,128)(2,1)S(1)}, f32[1,128]{1,0:T(1,128)S(1)}, f32[256,128]{1,0:T(8,128)S(1)}) custom-call(s32[128]{0:T(128)} %radii_hbm.1, bf16[78,128,128]{2,1,0:T(8,128)(2,1)} %bitcast.3, s32[78,128]{1,0:T(8,128)} %valid_hbm.1), custom_call_target="tpu_custom_call" | custom-call | tf_op jit(solution)/shard_map/pallas_call | solution.py:561
  45.2 1.5 %shard_map.59 = (bf16[78,128,128]{2,1,0:T(8,128)(2,1)}, f32[1,128]{1,0:T(1,128)}, f32[256,128]{1,0:T(8,128)}) custom-call(bf16[78,128,128]{2,1,0:T(8,128)(2,1)S(1)} %get-tuple-element.9.smoothed_ref, f32[1,128]{1,0:T(1,128)S(1)} %get-tuple-element.10.mean_ref, f32[256,128]{1,0:T(8,128)S(1)} %get-tuple-element.11.cov_ref), custom_call_target="tpu_custom_call" | custom-call | tf_op jit(solution)/shard_map/pallas_call | solution.py:603
